TPU v7x, 512 devices: a whole 4x8x8 slice. The times are simulated.
512 devices in a mesh: tile: 128 (over z, y, core), grp: 4 (over x).
Axes of the slice: x: 4, y: 8, z: 8, core: 2. Of those that a mesh axis runs over, the one named last changes fastest.
Arguments:
- kelvin_profile: float32 [90, 128, 256], P(None, 'tile'), may hold values from 0.5 to 1.5
- moisture_profile: float32 [90, 128, 256], P(None, 'tile'), may hold values from 0.1 to 3
- spreading_number: float32 [128, 256], P('tile'), may hold values from 0.05 to 0.24
- overhead_angle_measure: float32 [128, 256], P('tile'), may hold values from 0.2 to 1
- illuminated_mask: int32 [128, 256], P('tile'), may hold values 0 or 1
- radiating_tiles: int32 [32768, 1], P('tile'), may hold values from 0 to 127; in each aligned block of 256 rows (0 to 255, 256 to 511, ...) at most 4 rows name the same one
- cloudy_member_factors: float32 [224, 65536], P('grp', 'tile'), may hold values from 0.25 to 2
- arid_opacity_table: float32 [224, 90], P('grp'), may hold values from 0.003 to 0.2
- moisture_attenuation: float32 [224], P('grp'), may hold values from 0.003 to 0.05
- blackbody_share: float32 [224], P('grp'), may hold values from 0.3 to 3
- insolation_per_quadrature: float32 [224], P('grp'), may hold values from 0.3 to 3
Outputs:
- heating: float32 [90, 128, 256], P(None, 'tile')
- temp_next: float32 [90, 128, 256], P(None, 'tile')
- vapour_next: float32 [90, 128, 256], P(None, 'tile')
Inputs may be any that keep to these rules, and one draw needn't show every extreme that they name: `radiating_tiles`: among the columns of one tile no owner is named more than 4 times, a bound that some block reaches.
All inputs are finite; a program needn't handle non-finite values. No bound on the sum of `illuminated_mask` on one device may be relied on, other than what follows from the above.
Results may differ from a plain program's by a relative error of at most 0.00025.
Values sent between devices are 32-bit elements; how exact they have to be, the bound alone decides.
A program may use at most 64 MiB of HBM per device.

v0:
```python
import math
import jax
import jax.numpy as jnp
from jax import lax
from jax.sharding import PartitionSpec as P

NG = 224


def with_halo(block, sides, width):
    for axis, dim in sides:
        count = lax.axis_size(axis)
        forward = [(i, i + 1) for i in range(count - 1)]
        backward = [(target, source) for source, target in forward]
        low = lax.ppermute(
            lax.slice_in_dim(block, block.shape[dim] - width, None, axis=dim), axis, forward
        )
        high = lax.ppermute(lax.slice_in_dim(block, 0, width, axis=dim), axis, backward)
        block = jnp.concatenate([low, block, high], axis=dim)
    return block


def evaluate_warming(
    kelvin_profile,
    moisture_profile,
    overhead_angle_value,
    illuminated_marker,
    profile_window,
    arid_multiplier,
    moisture_multiplier,
    radiance_share_table,
    sunshine_multiplier,
):
    gpoints, strata_mesh = arid_multiplier.shape
    bundle = math.gcd(gpoints, 4)
    bundles = gpoints // bundle
    lower_mask = (jnp.arange(strata_mesh)[None, :] < jnp.arange(strata_mesh + 1)[:, None]).astype(
        jnp.float32
    )
    upper_mask = 1.0 - lower_mask

    def layer_pass(pieces):
        dry_part, vapour_part, radiance_share_piece, solar_part, sub_part = pieces
        thickness = (
            dry_part[:, :, None]
            + (vapour_part[:, None] * sub_part)[:, None, :] * moisture_profile[None]
        )
        column_depth = jnp.einsum(
            "lk,gkm->glm", lower_mask, thickness, precision=lax.Precision.HIGHEST
        )
        growth = jnp.exp(column_depth)
        damped = jnp.exp(-column_depth)
        infrared_radiance = radiance_share_piece[:, None, None] * kelvin_profile[None]
        downward = damped * jnp.einsum(
            "lk,gkm->glm",
            lower_mask,
            infrared_radiance * growth[:, :strata_mesh] * jnp.expm1(thickness),
            precision=lax.Precision.HIGHEST,
        )
        floor_term = infrared_radiance[:, strata_mesh - 1] * damped[:, strata_mesh]
        upward = growth * (
            floor_term[:, None, :]
            - jnp.einsum(
                "lk,gkm->glm",
                upper_mask,
                infrared_radiance * damped[:, :strata_mesh] * jnp.expm1(-thickness),
                precision=lax.Precision.HIGHEST,
            )
        )
        sunbeam = (
            solar_part[:, None, None]
            * illuminated_marker[None, None, :]
            * jnp.exp(-column_depth / overhead_angle_value[None, None, :])
        )
        fluxes = downward - upward + sunbeam
        return jnp.sum(fluxes[:, :strata_mesh] - fluxes[:, 1:], axis=0)

    spectral = lax.map(
        layer_pass,
        (
            arid_multiplier.reshape(bundles, bundle, strata_mesh),
            moisture_multiplier.reshape(bundles, bundle),
            radiance_share_table.reshape(bundles, bundle),
            sunshine_multiplier.reshape(bundles, bundle),
            profile_window.reshape(bundles, bundle, profile_window.shape[1]),
        ),
    )
    return jnp.sum(spectral, axis=0)


def advance(atmosphere_variables, spreading_number):
    padded = with_halo(atmosphere_variables, (("tile", 2),), 1)
    eastern = jnp.roll(atmosphere_variables, -1, axis=3)
    western = jnp.roll(atmosphere_variables, 1, axis=3)
    return atmosphere_variables + spreading_number * (
        padded[:, :, :-2] + padded[:, :, 2:] + eastern + western - 4.0 * atmosphere_variables
    )


def on_device(
    kelvin_profile,
    moisture_profile,
    spreading_number,
    overhead_angle_measure,
    illuminated_mask,
    radiating_tiles,
    cloudy_member_factors,
    arid_opacity_table,
    moisture_attenuation,
    blackbody_share,
    insolation_per_quadrature,
):
    strata_mesh, parallel_band_sequence, meridian_boxes = kelvin_profile.shape
    atmosphere_variables = jnp.stack([kelvin_profile, moisture_profile])
    for repeat in range(2):
        atmosphere_variables = advance(atmosphere_variables, spreading_number)
    temp_dyn = atmosphere_variables[0]
    vapour_next = atmosphere_variables[1]
    columns = parallel_band_sequence * meridian_boxes
    tile_count = lax.axis_size("tile")
    capacity = cloudy_member_factors.shape[1] // tile_count
    slots = tile_count * capacity
    owner_ids = radiating_tiles[:, 0]
    matches = (owner_ids[:, None] == jnp.arange(tile_count, dtype=jnp.int32)[None, :]).astype(
        jnp.int32
    )
    position = jnp.sum((jnp.cumsum(matches, axis=0) - 1) * matches, axis=1)
    slot_index = owner_ids * capacity + position
    overhead_angle_value = overhead_angle_measure.reshape(columns)
    sunlit_local = overhead_angle_value * illuminated_mask.reshape(columns).astype(jnp.float32)
    column_rows = jnp.concatenate(
        [temp_dyn.reshape(strata_mesh, columns).T, vapour_next.reshape(strata_mesh, columns).T],
        axis=1,
    )
    outgoing = (
        jnp.zeros((slots, 2 * strata_mesh), jnp.float32)
        .at[slot_index]
        .set(column_rows)
        .reshape(tile_count, capacity, 2 * strata_mesh)
    )
    sun_rows = jnp.stack([overhead_angle_value, sunlit_local], axis=1)
    blank = jnp.stack([jnp.ones((slots,), jnp.float32), jnp.zeros((slots,), jnp.float32)], axis=1)
    sun_out = blank.at[slot_index].set(sun_rows).reshape(tile_count, capacity, 2)
    incoming, sun_in = (
        lax.all_to_all(outgoing, "tile", split_axis=0, concat_axis=0, tiled=True),
        lax.all_to_all(sun_out, "tile", split_axis=0, concat_axis=0, tiled=True),
    )
    incoming = incoming.reshape(slots, 2 * strata_mesh)
    sun_in = sun_in.reshape(slots, 2)
    partial_value = evaluate_warming(
        incoming[:, :strata_mesh].T,
        incoming[:, strata_mesh:].T,
        sun_in[:, 0],
        sun_in[:, 1],
        cloudy_member_factors,
        arid_opacity_table,
        moisture_attenuation,
        blackbody_share,
        insolation_per_quadrature,
    )
    summed = lax.psum(partial_value, "grp")
    returning = lax.all_to_all(
        summed.T.reshape(tile_count, capacity, strata_mesh),
        "tile",
        split_axis=0,
        concat_axis=0,
        tiled=True,
    )
    total_heat = returning.reshape(slots, strata_mesh)[slot_index].T
    heating = (total_heat / NG).reshape(strata_mesh, parallel_band_sequence, meridian_boxes)
    return (heating, temp_dyn + heating, vapour_next)


def solution(mesh):
    in_specs = (
        P(None, "tile", None),
        P(None, "tile", None),
        P("tile", None),
        P("tile", None),
        P("tile", None),
        P("tile", None),
        P("grp", "tile"),
        P("grp", None),
        P("grp"),
        P("grp"),
        P("grp"),
    )
    out_specs = (P(None, "tile", None), P(None, "tile", None), P(None, "tile", None))
    return jax.shard_map(
        on_device, mesh=mesh, in_specs=in_specs, out_specs=out_specs, check_vma=False
    )
```

profile of v0, /device:TPU:1, one launch (start us, length us, event | category | flops | bytes accessed | tf_op | source)
XLA Modules:
  0.0 282.9 jit_solution(3957127956137913107)
XLA Ops:
  9.2 8.8 %collective-permute-start.1 = (f32[2,90,1,256]{1,3,2,0:T(8,128)S(1)}, f32[2,90,1,256]{1,3,2,0:T(8,128)S(1)}, u32[]{:S(2)}, u32[]{:S(2)}) collective-permute-start(f32[2,90,1,256]{1,3,2,0:T(8,128)S(1)} %pad_maximum_fusion), channel_id=1, source_target_pairs={{4,0},{8,4},{12,8},{16,12},{20,16},{24,20},{28,24},{32,28},{36,32}... | collective-permute-start | bytes 552968 | tf_op jit(solution)/shard_map/ppermute | solution.py:18
  18.0 1.9 collective-permute-start
  24.2 1.3 scatter_fusion
  25.5 1.5 copy.61
  27.0 12.7 %all-to-all-start.1 = ((f32[128,4,2]{1,2,0:T(2,128)}), f32[128,4,2]{1,2,0:T(2,128)S(1)}, u32[]{:S(2)}, u32[]{:S(2)}) async-start(f32[128,4,2]{1,2,0:T(2,128)} %copy.61), calls=%async_computation.1 | async-start | bytes 262144 | tf_op jit(solution)/shard_map/all_to_all | solution.py:146
  39.9 2.8 collective-permute-start.3
  42.7 2.8 collective-permute-start.2
  45.5 2.3 collective-permute-done.3
  48.9 1.7 scatter_custom_fusion
  52.4 15.6 %all-to-all-start = ((f32[128,4,180]{2,1,0:T(4,128)}), f32[128,4,180]{2,1,0:T(4,128)}, u32[]{:S(2)}, u32[]{:S(2)}) async-start(f32[128,4,180]{2,1,0:T(4,128)} %reshape.191), calls=%async_computation | async-start | bytes 1048576 | tf_op jit(solution)/shard_map/all_to_all | solution.py:145
  68.3 1.3 reshape.193
  69.7 1.3 reshape.194
  71.0 1.6 reshape.189
  74.2 14.0 %all-to-all-done = f32[128,4,180]{2,1,0:T(4,128)} async-done(((f32[128,4,180]{2,1,0:T(4,128)}), f32[128,4,180]{2,1,0:T(4,128)}, u32[]{:S(2)}, u32[]{:S(2)}) %all-to-all-start) | async-done | bytes 368672 | tf_op jit(solution)/shard_map/all_to_all | solution.py:145
  88.2 2.0 reshape.192
  90.2 2.0 slice_bitcast_fusion
  94.4 103.7 %while.12 = (s32[]{:T(128)}, f32[14,90,512]{2,1,0:T(8,128)S(1)}, f32[14,4,90]{2,1,0:T(4,128)}, f32[14,4]{1,0:T(8,128)S(1)}, f32[14,4,512]{2,1,0:T(4,128)}, /*ind...) while((s32[]{:T(128)}, f32[14,90,512]{2,1,0:T(8,128)S(1)}, ...), condition=%wide.region_7.8_spmd.clone.clone, body=%wide.region_5.7_spmd.clone.clone.sunk | while | flops 608476160 | bytes 12221821 | solution.py:78
  98.7 1.4 fusion.79
  100.2 1.5 fusion.81
  106.1 1.4 fusion.79
  107.6 1.5 fusion.81
  113.5 1.4 fusion.79
  115.0 1.5 fusion.81
  121.0 1.4 fusion.79
  122.4 1.5 fusion.81
  128.3 1.4 fusion.79
  129.8 1.5 fusion.81
  135.8 1.4 fusion.79
  137.2 1.5 fusion.81
  143.2 1.4 fusion.79
  144.6 1.5 fusion.81
  150.6 1.4 fusion.79
  152.0 1.5 fusion.81
  158.0 1.4 fusion.79
  159.4 1.5 fusion.81
  165.4 1.4 fusion.79
  166.8 1.5 fusion.81
  172.8 1.4 fusion.79
  174.2 1.5 fusion.81
  180.2 1.4 fusion.79
  181.6 1.5 fusion.81
  187.6 1.4 fusion.79
  189.0 1.5 fusion.81
  195.0 1.4 fusion.79
  196.4 1.5 fusion.81
  199.2 42.9 %all-reduce.2.cloned.1.call-done = f32[128,4,90]{2,1,0:T(4,128)} async-done(((f32[128,4,90]{2,1,0:T(4,128)}), f32[128,4,90]{2,1,0:T(4,128)}) %all-reduce.2.cloned.1.call-update) | async-done | bytes 184336 | tf_op jit(solution)/shard_map/psum | solution.py:161
  242.1 16.4 %all-to-all-start.2 = ((f32[128,4,90]{2,1,0:T(4,128)}), f32[128,4,90]{2,1,0:T(4,128)S(1)}, u32[]{:S(2)}, u32[]{:S(2)}) async-start(f32[128,4,90]{2,1,0:T(4,128)} %all-reduce.2.cloned.1.call-done), calls=%async_computation.2 | async-start | bytes 524288 | tf_op jit(solution)/shard_map/all_to_all | solution.py:162
  259.3 14.5 %all-to-all-done.2 = f32[128,4,90]{2,1,0:T(4,128)S(1)} async-done(((f32[128,4,90]{2,1,0:T(4,128)}), f32[128,4,90]{2,1,0:T(4,128)S(1)}, u32[]{:S(2)}, u32[]{:S(2)}) %all-to-all-start.2) | async-done | bytes 184352 | tf_op jit(solution)/shard_map/all_to_all | solution.py:162
  (249 shorter events, 78.8 us)
Async XLA Ops:
  7.2 17.0 %copy-start = (f32[512,2]{1,0:T(8,128)S(1)}, f32[512,2]{1,0:T(8,128)}, u32[]{:S(2)}) copy-start(f32[512,2]{1,0:T(8,128)} %constant.42.clone.1) | copy-start | bytes 12292
  9.2 30.5 %collective-permute-start.1 = (f32[2,90,1,256]{1,3,2,0:T(8,128)S(1)}, f32[2,90,1,256]{1,3,2,0:T(8,128)S(1)}, u32[]{:S(2)}, u32[]{:S(2)}) collective-permute-start(f32[2,90,1,256]{1,3,2,0:T(8,128)S(1)} %pad_maximum_fusion), channel_id=1, source_target_pairs={{4,0},{8,4},{12,8},{16,12},{20,16},{24,20},{28,24},{32,28},{36,32}... | collective-permute-start | bytes 552968 | tf_op jit(solution)/shard_map/ppermute | solution.py:18
  18.0 21.7 %collective-permute-start = (f32[2,90,1,256]{1,3,2,0:T(8,128)S(1)}, f32[2,90,1,256]{1,3,2,0:T(8,128)S(1)}, u32[]{:S(2)}, u32[]{:S(2)}) collective-permute-start(f32[2,90,1,256]{1,3,2,0:T(8,128)S(1)} %pad_maximum_fusion), channel_id=1, source_target_pairs={{0,4},{4,8},{8,12},{12,16},{16,20},{20,24},{24,28},{28,32},{32,36}... | collective-permute-start | bytes 552968 | tf_op jit(solution)/shard_map/ppermute | solution.py:15
  20.7 19.0 %copy-start.2 = (f32[1,256]{1,0:T(1,128)S(1)}, f32[1,256]{1,0:T(1,128)}, u32[]{:S(2)}) copy-start(f32[1,256]{1,0:T(1,128)} %param.15) | copy-start | bytes 3076
  27.0 25.5 %all-to-all-start.1 = ((f32[128,4,2]{1,2,0:T(2,128)}), f32[128,4,2]{1,2,0:T(2,128)S(1)}, u32[]{:S(2)}, u32[]{:S(2)}) async-start(f32[128,4,2]{1,2,0:T(2,128)} %copy.61), calls=%async_computation.1 | async-start | bytes 262144 | tf_op jit(solution)/shard_map/all_to_all | solution.py:146
  39.9 8.0 %collective-permute-start.3 = (f32[2,90,1,256]{1,3,2,0:T(8,128)S(1)}, f32[2,90,1,256]{1,3,2,0:T(8,128)S(1)}, u32[]{:S(2)}, u32[]{:S(2)}) collective-permute-start(f32[2,90,1,256]{1,3,2,0:T(8,128)S(1)} %fusion.45), channel_id=1, source_target_pairs={{4,0},{8,4},{12,8},{16,12},{20,16},{24,20},{28,24},{32,28},{36,32}... | collective-permute-start | bytes 552968 | tf_op jit(solution)/shard_map/ppermute | solution.py:18
  42.7 6.1 %collective-permute-start.2 = (f32[2,90,1,256]{1,3,2,0:T(8,128)S(1)}, f32[2,90,1,256]{1,3,2,0:T(8,128)S(1)}, u32[]{:S(2)}, u32[]{:S(2)}) collective-permute-start(f32[2,90,1,256]{1,3,2,0:T(8,128)S(1)} %fusion.45), channel_id=1, source_target_pairs={{0,4},{4,8},{8,12},{12,16},{16,20},{20,24},{24,28},{28,32},{32,36}... | collective-permute-start | bytes 552968 | tf_op jit(solution)/shard_map/ppermute | solution.py:15
  45.5 22.7 %copy-start.4 = (f32[56]{0:T(128)S(1)}, f32[56]{0:T(128)}, u32[]{:S(2)}) copy-start(f32[56]{0:T(128)} %param.21) | copy-start | bytes 676
  52.4 15.6 %copy-start.1 = (f32[128,4,2]{1,2,0:T(2,128)}, f32[128,4,2]{1,2,0:T(2,128)S(1)}, u32[]{:S(2)}) copy-start(f32[128,4,2]{1,2,0:T(2,128)S(1)} %all-to-all-done.1) | copy-start | bytes 12292
  52.4 35.8 %all-to-all-start = ((f32[128,4,180]{2,1,0:T(4,128)}), f32[128,4,180]{2,1,0:T(4,128)}, u32[]{:S(2)}, u32[]{:S(2)}) async-start(f32[128,4,180]{2,1,0:T(4,128)} %reshape.191), calls=%async_computation | async-start | bytes 1048576 | tf_op jit(solution)/shard_map/all_to_all | solution.py:145
  68.0 174.1 %all-reduce.2.cloned.1.call-start = ((), (), s32[]{:S(2)}) async-start(), calls=%async_computation.3 | async-start | bytes 524288 | tf_op jit(solution)/shard_map/psum | solution.py:161
  98.4 1.7 copy-start.3
  105.9 1.7 copy-start.3
  113.3 1.7 copy-start.3
  120.7 1.7 copy-start.3
  128.1 1.7 copy-start.3
  135.5 1.7 copy-start.3
  142.9 1.7 copy-start.3
  150.3 1.7 copy-start.3
  157.7 1.7 copy-start.3
  165.1 1.7 copy-start.3
  172.5 1.7 copy-start.3
  179.9 1.7 copy-start.3
  187.3 1.7 copy-start.3
  194.7 1.7 copy-start.3
  242.1 31.7 %all-to-all-start.2 = ((f32[128,4,90]{2,1,0:T(4,128)}), f32[128,4,90]{2,1,0:T(4,128)S(1)}, u32[]{:S(2)}, u32[]{:S(2)}) async-start(f32[128,4,90]{2,1,0:T(4,128)} %all-reduce.2.cloned.1.call-done), calls=%async_computation.2 | async-start | bytes 524288 | tf_op jit(solution)/shard_map/all_to_all | solution.py:162
Sparse Core Ops, SparseCore 0:
  199.4 42.6 all-reduce.1
where the time goes:
time: 286 us; the launch traced here: 283 us
  waiting for transfers between devices  75.5 us (26%)
  starting transfers between devices  61.2 us (21%)
  matrix products  54.1 us (19%)
  local copies, waits for them, and re-layouts  52.1 us (18%)
  other arithmetic  24.2 us (8%)
  between operations  14.3 us (5%)
    psum x1, waiting for transfers between devices, on_device(): summed = lax.psum(partial_value, 'grp')  42.9 us
    dot_general x14, matrix products, layer_pass(): jnp.einsum('lk,gkm->glm', lower_mask, infrared_radiance * growth[:, :stra...  21.2 us
    dot_general x14, matrix products, layer_pass(): jnp.einsum('lk,gkm->glm', upper_mask, infrared_radiance * damped[:, :stra...  19.8 us
    all_to_all x1, starting transfers between devices, on_device(): lax.all_to_all(summed.T.reshape(tile_count, capacity, strata_mesh), 'tile...  16.4 us
    all_to_all x1, starting transfers between devices, on_device(): lax.all_to_all(outgoing, 'tile', split_axis=0, concat_axis=0, tiled=True)  15.6 us
    all_to_all x1, waiting for transfers between devices, on_device(): lax.all_to_all(summed.T.reshape(tile_count, capacity, strata_mesh), 'tile...  14.5 us
    all_to_all x1, waiting for transfers between devices, on_device(): lax.all_to_all(outgoing, 'tile', split_axis=0, concat_axis=0, tiled=True)  14 us
    dot_general x14, matrix products, layer_pass(): jnp.einsum('lk,gkm->glm', lower_mask, thickness, precision=lax.Precision....  13.1 us
  transfers between devices with their start and end apart: 8, of which 6 were waited for; matrix products, arithmetic and copies ran while one was open for 6% of the time, Pallas kernels for 0%

commit v1 on v0

--- a/solution.py
+++ b/solution.py
@@ -3,6 +3,7 @@
 import jax.numpy as jnp
 from jax import lax
 from jax.sharding import PartitionSpec as P
+from jax.lax import axis_size, ppermute
 
 NG = 224
 
@@ -158,7 +159,15 @@
         blackbody_share,
         insolation_per_quadrature,
     )
-    summed = lax.psum(partial_value, "grp")
+    summed, z2 = (partial_value, 0)
+    n_all = axis_size("grp")
+    while 1 << z2 < n_all:
+        made = []
+        for idx in range(n_all):
+            made.append((idx, idx ^ 1 << z2))
+        z_new = ppermute(summed, "grp", perm=made)
+        summed = summed + z_new
+        z2 = z2 + 1
     returning = lax.all_to_all(
         summed.T.reshape(tile_count, capacity, strata_mesh),
         "tile",

time: 286 us -> 238 us (0.83)
  waiting for transfers between devices: 75.5 us -> 43.3 us
  between operations: 14.3 us -> 0.95 us
    psum x1 -> x0, waiting for transfers between devices: 42.9 us -> none  [on_device(): summed = lax.psum(partial_value, 'grp')]
    ppermute x0 -> x2, waiting for transfers between devices: none -> 10.4 us  [on_device(): z_new = ppermute(summed, 'grp', perm=made)]
    all_to_all x1, starting transfers between devices: 16.4 us -> 6.45 us  [on_device(): lax.all_to_all(summed.T.reshape(tile_count, capacity, strata_mesh), 'tile...]
    ppermute x0 -> x2, starting transfers between devices: none -> 7.76 us  [on_device(): z_new = ppermute(summed, 'grp', perm=made)]
  transfers between devices with their start and end apart: 8 -> 9, of which waited for: 6 -> 7; matrix products, arithmetic and copies ran while one was open for 6% -> 7% of each run, Pallas kernels for 0% -> 0%
where the time goes in v1:
time: 238 us; the launch traced here: 236 us
  starting transfers between devices  58.9 us (25%)
  matrix products  54.1 us (23%)
  local copies, waits for them, and re-layouts  52.8 us (22%)
  waiting for transfers between devices  43.3 us (18%)
  other arithmetic  24.3 us (10%)
    dot_general x14, matrix products, layer_pass(): jnp.einsum('lk,gkm->glm', lower_mask, infrared_radiance * growth[:, :stra...  21.2 us
    dot_general x14, matrix products, layer_pass(): jnp.einsum('lk,gkm->glm', upper_mask, infrared_radiance * damped[:, :stra...  19.8 us
    all_to_all x1, starting transfers between devices, on_device(): lax.all_to_all(outgoing, 'tile', split_axis=0, concat_axis=0, tiled=True)  15.7 us
    all_to_all x1, waiting for transfers between devices, on_device(): lax.all_to_all(summed.T.reshape(tile_count, capacity, strata_mesh), 'tile...  14.6 us
    all_to_all x1, waiting for transfers between devices, on_device(): lax.all_to_all(outgoing, 'tile', split_axis=0, concat_axis=0, tiled=True)  14.2 us
    dot_general x14, matrix products, layer_pass(): jnp.einsum('lk,gkm->glm', lower_mask, thickness, precision=lax.Precision....  13.1 us
    all_to_all x1, starting transfers between devices, on_device(): lax.all_to_all(sun_out, 'tile', split_axis=0, concat_axis=0, tiled=True)  12.7 us
    ppermute x2, starting transfers between devices, with_halo(): lax.ppermute(lax.slice_in_dim(block, 0, width, axis=dim), axis, backward)  11.6 us
  transfers between devices with their start and end apart: 9, of which 7 were waited for; matrix products, arithmetic and copies ran while one was open for 7% of the time, Pallas kernels for 0%

profile of v1, /device:TPU:1, one launch (start us, length us, event | category | flops | bytes accessed | tf_op | source)
XLA Modules:
  0.0 235.7 jit_solution(16176982722219651788)
XLA Ops:
  2.7 8.8 %collective-permute-start.1 = (f32[2,90,1,256]{1,3,2,0:T(8,128)S(1)}, f32[2,90,1,256]{1,3,2,0:T(8,128)S(1)}, u32[]{:S(2)}, u32[]{:S(2)}) collective-permute-start(f32[2,90,1,256]{1,3,2,0:T(8,128)S(1)} %pad_maximum_fusion), channel_id=1, source_target_pairs={{4,0},{8,4},{12,8},{16,12},{20,16},{24,20},{28,24},{32,28},{36,32}... | collective-permute-start | bytes 552968 | tf_op jit(solution)/shard_map/ppermute | solution.py:19
  11.5 1.9 collective-permute-start
  18.9 1.5 copy.61
  20.4 12.7 %all-to-all-start.1 = ((f32[128,4,2]{1,2,0:T(2,128)}), f32[128,4,2]{1,2,0:T(2,128)S(1)}, u32[]{:S(2)}, u32[]{:S(2)}) async-start(f32[128,4,2]{1,2,0:T(2,128)} %copy.61), calls=%async_computation.1 | async-start | bytes 262144 | tf_op jit(solution)/shard_map/all_to_all | solution.py:147
  33.4 2.8 %collective-permute-start.3 = (f32[2,90,1,256]{1,3,2,0:T(8,128)S(1)}, f32[2,90,1,256]{1,3,2,0:T(8,128)S(1)}, u32[]{:S(2)}, u32[]{:S(2)}) collective-permute-start(f32[2,90,1,256]{1,3,2,0:T(8,128)S(1)} %fusion.45), channel_id=1, source_target_pairs={{4,0},{8,4},{12,8},{16,12},{20,16},{24,20},{28,24},{32,28},{36,32}... | collective-permute-start | bytes 552968 | tf_op jit(solution)/shard_map/ppermute | solution.py:19
  36.2 2.8 %collective-permute-start.2 = (f32[2,90,1,256]{1,3,2,0:T(8,128)S(1)}, f32[2,90,1,256]{1,3,2,0:T(8,128)S(1)}, u32[]{:S(2)}, u32[]{:S(2)}) collective-permute-start(f32[2,90,1,256]{1,3,2,0:T(8,128)S(1)} %fusion.45), channel_id=1, source_target_pairs={{0,4},{4,8},{8,12},{12,16},{16,20},{20,24},{24,28},{28,32},{32,36}... | collective-permute-start | bytes 552968 | tf_op jit(solution)/shard_map/ppermute | solution.py:16
  39.0 2.3 collective-permute-done.3
  42.4 1.7 scatter_custom_fusion
  46.5 15.7 %all-to-all-start = ((f32[128,4,180]{2,1,0:T(4,128)}), f32[128,4,180]{2,1,0:T(4,128)}, u32[]{:S(2)}, u32[]{:S(2)}) async-start(f32[128,4,180]{2,1,0:T(4,128)} %reshape.191), calls=%async_computation | async-start | bytes 1048576 | tf_op jit(solution)/shard_map/all_to_all | solution.py:146
  65.0 1.6 reshape.189
  68.2 14.2 %all-to-all-done = f32[128,4,180]{2,1,0:T(4,128)} async-done(((f32[128,4,180]{2,1,0:T(4,128)}), f32[128,4,180]{2,1,0:T(4,128)}, u32[]{:S(2)}, u32[]{:S(2)}) %all-to-all-start) | async-done | bytes 368672 | tf_op jit(solution)/shard_map/all_to_all | solution.py:146
  82.4 2.0 reshape.192
  84.4 2.0 slice_bitcast_fusion
  88.6 103.7 %while.12 = (s32[]{:T(128)}, f32[14,90,512]{2,1,0:T(8,128)S(1)}, f32[14,4,90]{2,1,0:T(4,128)}, f32[14,4]{1,0:T(8,128)S(1)}, f32[14,4,512]{2,1,0:T(4,128)}, /*ind...) while((s32[]{:T(128)}, f32[14,90,512]{2,1,0:T(8,128)S(1)}, ...), condition=%wide.region_7.8_spmd.clone.clone, body=%wide.region_5.7_spmd.clone.clone.sunk | while | flops 608476160 | bytes 12221821 | solution.py:79
  92.9 1.4 fusion.79
  94.3 1.5 fusion.81
  100.3 1.4 fusion.79
  101.7 1.5 fusion.81
  107.7 1.4 fusion.79
  109.1 1.5 fusion.81
  115.1 1.4 fusion.79
  116.5 1.5 fusion.81
  122.5 1.4 fusion.79
  123.9 1.5 fusion.81
  129.9 1.4 fusion.79
  131.3 1.5 fusion.81
  137.3 1.4 fusion.79
  138.7 1.5 fusion.81
  144.7 1.4 fusion.79
  146.2 1.5 fusion.81
  152.1 1.4 fusion.79
  153.6 1.5 fusion.81
  159.5 1.4 fusion.79
  161.0 1.5 fusion.81
  166.9 1.4 fusion.79
  168.4 1.5 fusion.81
  174.3 1.4 fusion.79
  175.8 1.5 fusion.81
  181.7 1.4 fusion.79
  183.2 1.5 fusion.81
  189.1 1.4 fusion.79
  190.6 1.5 fusion.81
  192.5 3.1 %collective-permute-start.4 = (f32[90,512]{1,0:T(8,128)S(1)}, f32[90,512]{1,0:T(8,128)S(1)}, u32[]{:S(2)}, u32[]{:S(2)}) collective-permute-start(f32[90,512]{1,0:T(8,128)S(1)} %reduce_sum.31), channel_id=1, source_target_pairs={{0,1},{1,0},{2,3},{3,2},{4,5},{5,4},{6,7},{7,6},{8,9},{9,8},{10,11... | collective-permute-start | bytes 552968 | tf_op jit(solution)/shard_map/ppermute | solution.py:168
  195.7 5.6 %collective-permute-done.4 = f32[90,512]{1,0:T(8,128)S(1)} collective-permute-done((f32[90,512]{1,0:T(8,128)S(1)}, f32[90,512]{1,0:T(8,128)S(1)}, u32[]{:S(2)}, u32[]{:S(2)}) %collective-permute-start.4) | collective-permute-done | bytes 184352 | tf_op jit(solution)/shard_map/ppermute | solution.py:168
  201.3 4.6 %collective-permute-start.5 = (f32[90,512]{1,0:T(8,128)S(1)}, f32[90,512]{1,0:T(8,128)S(1)}, u32[]{:S(2)}, u32[]{:S(2)}) collective-permute-start(f32[90,512]{1,0:T(8,128)S(1)} %add.75), channel_id=1, source_target_pairs={{0,2},{1,3},{2,0},{3,1},{4,6},{5,7},{6,4},{7,5},{8,10},{9,11},{10,... | collective-permute-start | bytes 552968 | tf_op jit(solution)/shard_map/ppermute | solution.py:168
  206.0 4.8 %collective-permute-done.5 = f32[90,512]{1,0:T(8,128)S(1)} collective-permute-done((f32[90,512]{1,0:T(8,128)S(1)}, f32[90,512]{1,0:T(8,128)S(1)}, u32[]{:S(2)}, u32[]{:S(2)}) %collective-permute-start.5) | collective-permute-done | bytes 184352 | tf_op jit(solution)/shard_map/ppermute | solution.py:168
  211.6 6.5 %all-to-all-start.2 = ((f32[128,4,90]{2,1,0:T(4,128)}), f32[128,4,90]{2,1,0:T(4,128)S(1)}, u32[]{:S(2)}, u32[]{:S(2)}) async-start(f32[128,4,90]{2,1,0:T(4,128)} %bitcast.21), calls=%async_computation.2 | async-start | bytes 524288 | tf_op jit(solution)/shard_map/all_to_all | solution.py:171
  218.8 14.6 %all-to-all-done.2 = f32[128,4,90]{2,1,0:T(4,128)S(1)} async-done(((f32[128,4,90]{2,1,0:T(4,128)}), f32[128,4,90]{2,1,0:T(4,128)S(1)}, u32[]{:S(2)}, u32[]{:S(2)}) %all-to-all-start.2) | async-done | bytes 184352 | tf_op jit(solution)/shard_map/all_to_all | solution.py:171
  (252 shorter events, 83.1 us)
Async XLA Ops:
  0.6 17.0 %copy-start = (f32[512,2]{1,0:T(8,128)S(1)}, f32[512,2]{1,0:T(8,128)}, u32[]{:S(2)}) copy-start(f32[512,2]{1,0:T(8,128)} %constant.42.clone.1) | copy-start | bytes 12292
  2.7 30.5 %collective-permute-start.1 = (f32[2,90,1,256]{1,3,2,0:T(8,128)S(1)}, f32[2,90,1,256]{1,3,2,0:T(8,128)S(1)}, u32[]{:S(2)}, u32[]{:S(2)}) collective-permute-start(f32[2,90,1,256]{1,3,2,0:T(8,128)S(1)} %pad_maximum_fusion), channel_id=1, source_target_pairs={{4,0},{8,4},{12,8},{16,12},{20,16},{24,20},{28,24},{32,28},{36,32}... | collective-permute-start | bytes 552968 | tf_op jit(solution)/shard_map/ppermute | solution.py:19
  11.5 21.7 %collective-permute-start = (f32[2,90,1,256]{1,3,2,0:T(8,128)S(1)}, f32[2,90,1,256]{1,3,2,0:T(8,128)S(1)}, u32[]{:S(2)}, u32[]{:S(2)}) collective-permute-start(f32[2,90,1,256]{1,3,2,0:T(8,128)S(1)} %pad_maximum_fusion), channel_id=1, source_target_pairs={{0,4},{4,8},{8,12},{12,16},{16,20},{20,24},{24,28},{28,32},{32,36}... | collective-permute-start | bytes 552968 | tf_op jit(solution)/shard_map/ppermute | solution.py:16
  14.2 19.0 %copy-start.2 = (f32[1,256]{1,0:T(1,128)S(1)}, f32[1,256]{1,0:T(1,128)}, u32[]{:S(2)}) copy-start(f32[1,256]{1,0:T(1,128)} %param.15) | copy-start | bytes 3076
  20.4 25.4 %all-to-all-start.1 = ((f32[128,4,2]{1,2,0:T(2,128)}), f32[128,4,2]{1,2,0:T(2,128)S(1)}, u32[]{:S(2)}, u32[]{:S(2)}) async-start(f32[128,4,2]{1,2,0:T(2,128)} %copy.61), calls=%async_computation.1 | async-start | bytes 262144 | tf_op jit(solution)/shard_map/all_to_all | solution.py:147
  33.4 8.0 %collective-permute-start.3 = (f32[2,90,1,256]{1,3,2,0:T(8,128)S(1)}, f32[2,90,1,256]{1,3,2,0:T(8,128)S(1)}, u32[]{:S(2)}, u32[]{:S(2)}) collective-permute-start(f32[2,90,1,256]{1,3,2,0:T(8,128)S(1)} %fusion.45), channel_id=1, source_target_pairs={{4,0},{8,4},{12,8},{16,12},{20,16},{24,20},{28,24},{32,28},{36,32}... | collective-permute-start | bytes 552968 | tf_op jit(solution)/shard_map/ppermute | solution.py:19
  36.2 6.1 %collective-permute-start.2 = (f32[2,90,1,256]{1,3,2,0:T(8,128)S(1)}, f32[2,90,1,256]{1,3,2,0:T(8,128)S(1)}, u32[]{:S(2)}, u32[]{:S(2)}) collective-permute-start(f32[2,90,1,256]{1,3,2,0:T(8,128)S(1)} %fusion.45), channel_id=1, source_target_pairs={{0,4},{4,8},{8,12},{12,16},{16,20},{20,24},{24,28},{28,32},{32,36}... | collective-permute-start | bytes 552968 | tf_op jit(solution)/shard_map/ppermute | solution.py:16
  39.0 23.2 %copy-start.4 = (f32[56]{0:T(128)S(1)}, f32[56]{0:T(128)}, u32[]{:S(2)}) copy-start(f32[56]{0:T(128)} %param.21) | copy-start | bytes 676
  45.8 0.7 copy-start.1
  46.5 35.9 %all-to-all-start = ((f32[128,4,180]{2,1,0:T(4,128)}), f32[128,4,180]{2,1,0:T(4,128)}, u32[]{:S(2)}, u32[]{:S(2)}) async-start(f32[128,4,180]{2,1,0:T(4,128)} %reshape.191), calls=%async_computation | async-start | bytes 1048576 | tf_op jit(solution)/shard_map/all_to_all | solution.py:146
  92.6 1.7 copy-start.3
  100.0 1.7 copy-start.3
  107.4 1.7 copy-start.3
  114.8 1.7 copy-start.3
  122.2 1.7 copy-start.3
  129.6 1.7 copy-start.3
  137.0 1.7 copy-start.3
  144.4 1.7 copy-start.3
  151.8 1.7 copy-start.3
  159.2 1.7 copy-start.3
  166.6 1.7 copy-start.3
  174.1 1.7 copy-start.3
  181.5 1.7 copy-start.3
  188.9 1.7 copy-start.3
  192.5 8.8 %collective-permute-start.4 = (f32[90,512]{1,0:T(8,128)S(1)}, f32[90,512]{1,0:T(8,128)S(1)}, u32[]{:S(2)}, u32[]{:S(2)}) collective-permute-start(f32[90,512]{1,0:T(8,128)S(1)} %reduce_sum.31), channel_id=1, source_target_pairs={{0,1},{1,0},{2,3},{3,2},{4,5},{5,4},{6,7},{7,6},{8,9},{9,8},{10,11... | collective-permute-start | bytes 552968 | tf_op jit(solution)/shard_map/ppermute | solution.py:168
  201.3 9.4 %collective-permute-start.5 = (f32[90,512]{1,0:T(8,128)S(1)}, f32[90,512]{1,0:T(8,128)S(1)}, u32[]{:S(2)}, u32[]{:S(2)}) collective-permute-start(f32[90,512]{1,0:T(8,128)S(1)} %add.75), channel_id=1, source_target_pairs={{0,2},{1,3},{2,0},{3,1},{4,6},{5,7},{6,4},{7,5},{8,10},{9,11},{10,... | collective-permute-start | bytes 552968 | tf_op jit(solution)/shard_map/ppermute | solution.py:168
  211.6 21.8 %all-to-all-start.2 = ((f32[128,4,90]{2,1,0:T(4,128)}), f32[128,4,90]{2,1,0:T(4,128)S(1)}, u32[]{:S(2)}, u32[]{:S(2)}) async-start(f32[128,4,90]{2,1,0:T(4,128)} %bitcast.21), calls=%async_computation.2 | async-start | bytes 524288 | tf_op jit(solution)/shard_map/all_to_all | solution.py:171
